TPU v7x, 32 devices: a whole 2x2x4 slice. The times are simulated.
32 devices in a mesh: groups: 2 (over y), replica: 4 (over z), sx: 4 (over x, core).
Axes of the slice: x: 2, y: 2, z: 4, core: 2. Of those that a mesh axis runs over, the one named last changes fastest.
Arguments:
- coords: float32 [3, 8, 4096], P(None, ('groups', 'replica'), 'sx'), parts along dimension 1, may hold values from 0 to 1
- widths: float32 [8, 4096], P(('groups', 'replica'), 'sx'), parts along dimension 0, may hold values from 1 to 2
- amplitudes: float32 [8, 4096], P(('groups', 'replica'), 'sx'), parts along dimension 0, may hold values from 1 to 4
- live_blocks: int32 [8, 4], P(('groups', 'replica'), 'sx'), parts along dimension 0, may hold values from 1 to 8, as said below
- target_map: float32 [192, 64, 480], P(('groups', 'sx')), parts along dimension 0, may hold values from -2 to 2
Outputs:
- mean_density: float32 [192, 64, 480], P(('groups', 'sx'), 'replica'), parts along dimension 0
- forces: float32 [3, 8, 4096], P(None, ('groups', 'replica'), 'sx'), parts along dimension 1
There are 2 independent parts, one for each index of `groups`. A program takes and returns all parts, laid end to end along the dimension named above; each array names one. Nothing has to cross between parts.
Inputs may be any that keep to these rules, and one draw needn't show every extreme that they name: `live_blocks`: blocks past the count hold padding slots. Some member's brick has all 8 blocks in use in every draw.
All inputs are finite; a program needn't handle non-finite values.
Results may differ from a plain program's by a relative error of at most 0.0044.
Values may be sent and summed in bfloat16 or wider, within the bound.
No kernel may reach another device: no remote copies, remote signals or barrier semaphores. Data moves between devices by JAX's collectives and lax.ppermute only.
A program may use at most 64 MiB of HBM per device.

v0:
```python
import functools
import math

import jax
import jax.numpy as jnp
from jax import lax
from jax.experimental import pallas as pl
from jax.experimental.pallas import tpu as pltpu
from jax.sharding import PartitionSpec as P

CX = 24
NZ = 64
NY = 480
REACH = 6
BLOCK = 128
BLOCKS = 8
ATOMS_DEV = 1024
SPAN = CX + 2 * REACH
LAP = 2 * REACH
LANES = 512
FIELDS = 5
HALF_LOG2E = 0.5 * math.log2(math.e)
STASH_LIMIT = 4

noise_floor = 0.05


def pack_kernel(coords_ref, widths_ref, amplitudes_ref, live_ref, own_ref, sems):
    copies = [
        pltpu.make_async_copy(coords_ref, own_ref.at[pl.ds(0, 3)], sems.at[0]),
        pltpu.make_async_copy(widths_ref, own_ref.at[3], sems.at[1]),
        pltpu.make_async_copy(amplitudes_ref, own_ref.at[4], sems.at[2]),
    ]
    for copy in copies:
        copy.start()
    for copy in copies:
        copy.wait()
    block = lax.broadcasted_iota(jnp.int32, (BLOCKS, BLOCK), 0)
    own_ref[4] = jnp.where(block < live_ref[0, 0], own_ref[4], 0.0)


def live_of(ref, member):
    number = (lax.broadcasted_iota(jnp.int32, (BLOCKS, BLOCK), 0) + 1).astype(jnp.float32)
    return jnp.max(jnp.where(ref[member, 4] != 0.0, number, 0.0)).astype(jnp.int32)


def split(code):
    return lax.shift_right_logical(code, 3), code & 7


def listed(out, count, first, stride, base, live):
    for block in range(first, BLOCKS, stride):
        out[count] = base + block
        count = count + jnp.where(block < live, 1, 0)
    return count


class Tables:
    def __init__(self, zp, zs, atoms_ref):
        self.zp, self.zs, self.atoms_ref = zp, zs, atoms_ref
        self.brick = lax.axis_index("sx")
        self.last_plane = CX * lax.axis_size("sx")
        self.step = lax.broadcasted_iota(jnp.int32, (16, BLOCK), 0).astype(jnp.float32)
        step_z = lax.broadcasted_iota(jnp.int32, (zp, BLOCK), 0)
        self.own_z = (step_z < zs).astype(jnp.float32)
        self.cell_z = (step_z + lax.axis_index("replica") * zs).astype(jnp.float32)

    def fields(self, data):
        frac_x, frac_y, frac_z, width, weight = data
        inv = 1.0 / width
        q = inv * inv
        return frac_x, frac_y, frac_z, q, q * -HALF_LOG2E, weight

    def own_fields(self, member, block):
        return self.fields([self.atoms_ref[member, f, pl.ds(block, 1), :] for f in range(FIELDS)])

    def y(self, out, slopes, frac, power, q):
        base = self.step - NY * frac
        for k in range(NY // 16):
            off = base + float(16 * k)
            value = jnp.exp2(off * off * power)
            out[16 * k : 16 * k + 16, :] = value.astype(jnp.bfloat16)
            if slopes is not None:
                slopes[16 * k : 16 * k + 16, :] = (value * (off * q)).astype(jnp.bfloat16)

    def x(self, frac, power, shift, lower, count, edges):
        cell = lax.broadcasted_iota(jnp.int32, (count, BLOCK), 0) + lower
        off = cell.astype(jnp.float32) - (CX * frac + shift)
        value = jnp.exp2(off * off * power)
        if edges:
            plane = cell + (self.brick * CX - REACH)
            value = jnp.where((plane >= 0) & (plane < self.last_plane), value, 0.0)
        return value, off

    def z(self, frac, power):
        off = self.cell_z - NZ * frac
        value = jnp.exp2(off * off * power)
        return (value if self.zs == self.zp else value * self.own_z), off


def zero_tails(*tables):
    for table in tables:
        table[:, NY:, :] = jnp.zeros((table.shape[0], LANES - NY, BLOCK), jnp.bfloat16)


def splat_kernel(
    members, zp, zs, sliced, stash, atoms_ref, near_ref, far_ref, target_ref, rho, wanted, *rest
):
    if stash:
        gy, slope, gy_side, sides, more_list, side_list, sem = rest
    else:
        gy, gy_side, sides, more_list, side_list, sem = rest
        slope = None
    odd = lax.rem(lax.axis_index("sx"), 2)
    if sliced:
        z_first = pl.multiple_of(lax.axis_index("replica") * zs, 8)
        source = target_ref.at[:, pl.ds(z_first, zs), :]
    else:
        source = target_ref
    fetch = pltpu.make_async_copy(source, wanted, sem)
    fetch.start()

    brick = lax.axis_index("sx")
    inner = (brick > 0) & (brick < lax.axis_size("sx") - 1)

    def list_member(member, counts):
        own, near, far = (live_of(ref, member) for ref in (atoms_ref, near_ref, far_ref))
        far = jnp.where(inner, far, 0)
        base = member * BLOCKS
        sides[member] = near_ref[member]
        sides[members + member] = far_ref[member]
        side_count = listed(side_list, counts[1], 0, 1, base, near)
        return (
            listed(more_list, counts[0], 2, 2, base, own),
            listed(side_list, side_count, 0, 1, members * BLOCKS + base, far),
        )

    more_count, side_count = lax.fori_loop(
        0, members, list_member, (jnp.int32(0),) * 2, unroll=members <= 4
    )
    zero_tails(gy, gy_side)
    if stash:
        zero_tails(slope)
    tables = Tables(zp, zs, atoms_ref)

    def left_of(scaled, gz, count):
        group = max(1, 16 // zp)
        made = []
        for t in range(0, count, group):
            pieces = [scaled[t + i : t + i + 1] * gz for i in range(group)]
            piece = pieces[0] if group == 1 else jnp.concatenate(pieces, 0)
            made.append(piece.astype(jnp.bfloat16))
        return jnp.concatenate(made, 0)

    def matmul_t(a, b):
        return lax.dot_general(a, b, (((1,), (1,)), ((), ())), preferred_element_type=jnp.float32)

    def own_splat(member, block, part):
        at = [member * BLOCKS + block + half if stash else 2 * part + half for half in range(2)]
        lefts = []
        for half in range(2):
            frac_x, frac_y, frac_z, q, power, weight = tables.own_fields(member, block + half)
            gx, _ = tables.x(frac_x, power, REACH, 0, SPAN, True)
            gz, _ = tables.z(frac_z, power)
            tables.y(gy.at[at[half]], slope.at[at[half]] if stash else None, frac_y, power, q)
            lefts.append(left_of(weight * gx, gz, SPAN))
        return matmul_t(
            jnp.concatenate(lefts, 1),
            jnp.concatenate([gy[at[0]], gy[at[1]]], 1),
        )

    def start_members(step_at, carry):
        for part in range(start_group):
            member = start_group * step_at + part
            rho[member] = own_splat(member, 0, part)
        return carry

    start_group = min(members, 4)
    lax.fori_loop(0, members // start_group, start_members, 0)

    def more_pair(unit, part):
        code = more_list[unit]
        member, block = split(code)
        rho[member] += own_splat(member, block, part)

    side_group = gy_side.shape[0]

    def side_units(step_at):
        for part in range(side_group):
            unit = side_group * step_at + part
            code = side_list[jnp.minimum(unit, side_count - 1)]
            place, block = split(code)
            is_near = place < members
            member = jnp.where(is_near, place, place - members)
            above = jnp.where(is_near, 1 - odd, odd)
            block = pl.ds(block, 1)
            keep = jnp.where(unit < side_count, 1.0, 0.0)
            lower = CX * above
            shift = (REACH - CX + 2 * CX * above).astype(jnp.float32)
            frac_x, frac_y, frac_z, q, power, weight = tables.fields(
                [sides[place, f, block, :] for f in range(FIELDS)]
            )
            gx, _ = tables.x(frac_x, power, shift, lower, LAP, False)
            gz, _ = tables.z(frac_z, power)
            tables.y(gy_side.at[part], None, frac_y, power, q)
            side_left = left_of(weight * keep * gx, gz, LAP)
            at = pl.ds(pl.multiple_of(lower * zp, 16), LAP * zp)
            rho[member, at, :] += matmul_t(side_left, gy_side[part])

    def both(step_at, carry):
        more_pair(step_at, 0)
        side_units(step_at)
        return carry

    def more_alone(step_at, carry):
        more_pair(step_at, 0)
        return carry

    def side_alone(step_at, carry):
        side_units(step_at)
        return carry

    side_steps = (side_count + side_group - 1) // side_group
    shared = jnp.minimum(more_count, side_steps)
    lax.fori_loop(0, shared, both, 0)
    lax.fori_loop(shared, more_count, more_alone, 0)
    lax.fori_loop(shared, side_steps, side_alone, 0)
    fetch.wait()


def pull_kernel(members, zp, zs, stash, atoms_ref, near_target, far_target, rho, wanted, *rest):
    if stash:
        gy, slope, *rest = rest
        mean_ref, *outs, grad, mean_vmem, pulled, rows, forces, pull_list, sem = rest
    else:
        mean_ref, *outs, grad, mean_vmem, pulled, rows, forces, pull_list, sem, gy, slope = rest
    odd = lax.rem(lax.axis_index("sx"), 2)

    def list_member(member, count):
        return listed(pull_list, count, 0, 1, member * BLOCKS, live_of(atoms_ref, member))

    pull_count = lax.fori_loop(0, members, list_member, jnp.int32(0), unroll=members <= 4)
    forces[...] = jnp.zeros_like(forces)
    grad[:, :, NY - 96 :] = jnp.zeros((members, SPAN * zp, LANES - NY + 96), jnp.bfloat16)
    if not stash:
        zero_tails(gy, slope)
    tables = Tables(zp, zs, atoms_ref)

    group = max(1, 16 // zp)

    def gradient(first_plane, goal, means, t, carry):
        at = pl.ds(pl.multiple_of((first_plane + t * group) * zp, 16), group * zp)
        planes = pl.ds(t * group, group)
        here = [rho[m, at, 0:NY] for m in range(members)]
        first = functools.reduce(jnp.add, here)
        second = functools.reduce(jnp.add, [f * f for f in here])
        mean = first * (1.0 / members)
        spread = second * (1.0 / members) - mean * mean
        noise = noise_floor + spread * (1.0 / members)
        guess = pl.reciprocal(noise, approx=True)
        inv = guess * (2.0 - noise * guess)
        pull = (goal[planes].reshape(group * zp, NY) - mean) * inv
        gain = (inv - pull * pull) * (1.0 / (members * members))
        offset = pull * (-1.0 / members) - gain * mean
        for m in range(members):
            grad[m, at, 0:NY] = (offset + gain * here[m]).astype(jnp.bfloat16)
        if means is not None:
            means[planes] = mean.reshape(group, zp, NY)
        return carry

    for first_plane, goal, means in (
        (REACH, wanted, mean_vmem),
        ((REACH + CX) * (1 - odd), near_target, None),
        ((REACH + CX) * odd, far_target, None),
    ):
        steps = goal.shape[0] // group
        lax.fori_loop(0, steps, functools.partial(gradient, first_plane, goal, means), 0, unroll=3)
    give = pltpu.make_async_copy(mean_vmem, mean_ref, sem)
    give.start()

    pull_group = pulled.shape[0]

    def pull_units(first_unit, units):
        for part in range(units):
            code = pull_list[jnp.minimum(first_unit + part, pull_count - 1)]
            member, block = split(code)
            frac_x, frac_y, frac_z, q, power, weight = tables.own_fields(member, block)
            gx, off_x = tables.x(frac_x, power, REACH, 0, SPAN, True)
            gz, off_z = tables.z(frac_z, power)
            rows[part, 0:SPAN] = gx
            rows[part, SPAN : 2 * SPAN] = gx * off_x * q
            slot = code if stash else part
            if not stash:
                tables.y(gy.at[slot], slope.at[slot], frac_y, power, q)
            got = jnp.dot(
                grad[member], jnp.concatenate([gy[slot], slope[slot]], 1),
                preferred_element_type=jnp.float32,
            )
            sum_x = jnp.zeros((zp, BLOCK), jnp.float32)
            sum_y = jnp.zeros((zp, BLOCK), jnp.float32)
            sum_z = jnp.zeros((zp, BLOCK), jnp.float32)
            for t in range(SPAN):
                plain = got[t * zp : (t + 1) * zp, 0:BLOCK]
                slanted = got[t * zp : (t + 1) * zp, BLOCK:]
                here = rows[part, t : t + 1]
                sum_x += rows[part, SPAN + t : SPAN + t + 1] * plain
                sum_y += here * slanted
                sum_z += here * plain
            at = pl.ds(block, 1)
            forces[member, 0, at] = weight * jnp.sum(sum_x * gz, 0, keepdims=True)
            forces[member, 1, at] = weight * jnp.sum(sum_y * gz, 0, keepdims=True)
            forces[member, 2, at] = weight * jnp.sum(sum_z * (gz * off_z * q), 0, keepdims=True)

    def pull_many(step_at, carry):
        pull_units(pull_group * step_at, pull_group)
        return carry

    def pull_two(step_at, carry):
        pull_units(2 * step_at, 2)
        return carry

    def pull_four(step_at, carry):
        pull_units(4 * step_at, 4)
        return carry

    eights = lax.shift_right_logical(pull_count, 3)
    fours = lax.shift_right_logical(pull_count, 2)
    lax.fori_loop(0, eights, pull_many, 0)
    lax.fori_loop(2 * eights, fours, pull_four, 0)
    lax.fori_loop(2 * fours, lax.shift_right_logical(pull_count + 1, 1), pull_two, 0)
    if len(outs) == 1:
        outs[0][...] = forces[...]
    else:
        for k, out in enumerate(outs):
            out[...] = forces[k]
    give.wait()


def shards(coords, widths, amplitudes, live_blocks, target_map):
    members = lax.axis_size("replica")
    bricks = lax.axis_size("sx")
    rank = lax.axis_index("replica")
    zs = NZ // members
    zp = max(zs, 8)
    sliced = zs % 8 == 0
    few = members <= 4 and members & (members - 1) == 0
    stash = members <= STASH_LIMIT
    blocks = (BLOCKS, BLOCK)
    vmem = pl.BlockSpec(memory_space=pltpu.VMEM)
    anywhere = pl.BlockSpec(memory_space=pl.ANY)

    target = target_map
    if not sliced:
        part = lax.dynamic_slice_in_dim(target_map, rank * zs, zs, 1)
        target = jnp.pad(part, ((0, 0), (0, zp - zs), (0, 0)))
    hbm = pl.BlockSpec(memory_space=pltpu.HBM)
    own = pl.pallas_call(
        pack_kernel,
        out_shape=jax.ShapeDtypeStruct((FIELDS,) + blocks, jnp.float32),
        in_specs=[hbm] * 3 + [pl.BlockSpec(memory_space=pltpu.SMEM)],
        out_specs=vmem,
        scratch_shapes=[pltpu.SemaphoreType.DMA((3,))],
        compiler_params=pltpu.CompilerParams(vmem_limit_bytes=4 * 1024 * 1024),
        name="pack",
    )(
        *(
            pltpu.with_memory_space_constraint(x, pltpu.HBM)
            for x in (coords.reshape((3,) + blocks), widths.reshape(blocks), amplitudes.reshape(blocks))
        ),
        live_blocks,
    )

    odd = lax.rem(lax.axis_index("sx"), 2)

    def edge(plane):
        z_first = rank * zs if sliced else 0
        return lax.dynamic_slice(target, (plane, z_first, 0), (REACH, zp, NY))

    near_edge, far_edge = edge((CX - REACH) * (1 - odd)), edge((CX - REACH) * odd)

    def swap(block, pairs):
        return lax.ppermute(block, "sx", pairs + [(b, a) for a, b in pairs])

    near_pairs = [(i, i + 1) for i in range(0, bricks - 1, 2)]
    far_pairs = [(i, i + 1) for i in range(1, bricks - 1, 2)]
    if bricks % 2 == 0 and bricks > 2:
        far_pairs.append((bricks - 1, 0))

    def across(block, k):
        return lax.ppermute(block, "replica", [(i, i ^ k) for i in range(members)])

    if few:
        got = {0: own}
        for k in (2, 3, 1):
            got[k] = across(own, k)
        everyone = jnp.stack([got[k] for k in range(members)])
        everyone, near_edge, far_edge = lax.optimization_barrier((everyone, near_edge, far_edge))
    else:
        everyone = lax.all_gather(own, "replica")
    far, near = swap(everyone, far_pairs), swap(everyone, near_pairs)
    near_edge, far_edge, _ = lax.optimization_barrier((near_edge, far_edge, everyone))
    far_target, near_target = swap(far_edge, far_pairs), swap(near_edge, near_pairs)

    force_shapes = (
        [jax.ShapeDtypeStruct((3,) + blocks, jnp.float32)] * members
        if few
        else [jax.ShapeDtypeStruct((members, 3) + blocks, jnp.float32)]
    )
    table = ((members * BLOCKS if stash else 8), LANES, BLOCK)
    tables = [jax.ShapeDtypeStruct(table, jnp.bfloat16)] * 2 if stash else []
    splat = pl.pallas_call(
        functools.partial(splat_kernel, members, zp, zs, sliced, stash),
        out_shape=[
            jax.ShapeDtypeStruct((members, SPAN * zp, LANES), jnp.float32),
            jax.ShapeDtypeStruct((CX, zp, NY), jnp.float32),
        ]
        + tables,
        in_specs=[vmem] * 3 + [hbm],
        out_specs=[vmem] * (2 + len(tables)),
        scratch_shapes=([] if stash else [pltpu.VMEM(table, jnp.bfloat16)])
        + [
            pltpu.VMEM((4, LANES, BLOCK), jnp.bfloat16),
            pltpu.VMEM((2 * members, FIELDS) + blocks, jnp.float32),
            pltpu.SMEM((members * BLOCKS + 1,), jnp.int32),
            pltpu.SMEM((2 * members * BLOCKS + 1,), jnp.int32),
            pltpu.SemaphoreType.DMA,
        ],
        compiler_params=pltpu.CompilerParams(vmem_limit_bytes=24 * 1024 * 1024),
        cost_estimate=pl.CostEstimate(flops=6_000_000_000, bytes_accessed=14_000_000, transcendentals=0),
        name="splat",
    )(everyone, near, far, pltpu.with_memory_space_constraint(target, pltpu.HBM))
    mean, *partial = pl.pallas_call(
        functools.partial(pull_kernel, members, zp, zs, stash),
        out_shape=[jax.ShapeDtypeStruct((CX, zp, NY), jnp.float32)] + force_shapes,
        in_specs=[vmem] * (3 + len(splat)),
        out_specs=[anywhere] + [vmem] * len(force_shapes),
        scratch_shapes=[
            pltpu.VMEM((members, SPAN * zp, LANES), jnp.bfloat16),
            pltpu.VMEM((CX, zp, NY), jnp.float32),
            pltpu.VMEM((8, SPAN * zp, 2 * BLOCK), jnp.float32),
            pltpu.VMEM((8, 2 * SPAN, BLOCK), jnp.float32),
            pltpu.VMEM((members, 3) + blocks, jnp.float32),
            pltpu.SMEM((members * BLOCKS + 1,), jnp.int32),
            pltpu.SemaphoreType.DMA,
        ]
        + ([] if stash else [pltpu.VMEM(table, jnp.bfloat16)] * 2),
        compiler_params=pltpu.CompilerParams(vmem_limit_bytes=(24 if stash else 40) * 1024 * 1024),
        cost_estimate=pl.CostEstimate(flops=6_000_000_000, bytes_accessed=14_000_000, transcendentals=0),
        name="pull",
    )(everyone, near_target, far_target, *splat)

    if few:
        forces = partial[0]
        for k in (2, 3, 1):
            forces = forces + across(partial[k], k)
    else:
        forces = lax.psum_scatter(partial[0], "replica", scatter_dimension=0)
    return mean[:, :zs], forces.reshape(3, 1, ATOMS_DEV)


def solution(mesh):
    placed = (
        P(None, ("groups", "replica"), "sx"),
        P(("groups", "replica"), "sx"),
        P(("groups", "replica"), "sx"),
        P(("groups", "replica"), "sx"),
        P(("groups", "sx"), None, None),
    )
    return jax.shard_map(
        shards,
        mesh=mesh,
        in_specs=placed,
        out_specs=(P(("groups", "sx"), "replica", None), P(None, ("groups", "replica"), "sx")),
        check_vma=False,
    )
```

profile of v0, /device:TPU:1, one launch (start us, length us, event | category | flops | bytes accessed | tf_op | source)
XLA Modules:
  0.0 34.3 jit_solution(10789034071850691152)
XLA Ops:
  1.3 0.7 %pack.1 = f32[5,8,128]{2,1,0:T(8,128)S(1)} custom-call(f32[3,8,128]{2,1,0:T(8,128)} %bitcast.12, f32[8,128]{1,0:T(8,128)} %bitcast.14, f32[8,128]{1,0:T(8,128)} %bitcast.15, s32[1,1]{1,0:T(1,128)S(6)} %copy.9.live_ref), custom_call_target="tpu_custom_call" | custom-call | tf_op jit(solution)/shard_map/pack/pallas_call | solution.py:357
  2.0 4.2 %collective-permute-start.2 = (f32[5,8,128]{2,1,0:T(8,128)S(1)}, f32[5,8,128]{2,1,0:T(8,128)S(1)}, u32[]{:S(2)}, u32[]{:S(2)}) collective-permute-start(f32[5,8,128]{2,1,0:T(8,128)S(1)} %pack.1), channel_id=1, source_target_pairs={{0,12},{4,8},{8,4},{12,0},{1,13},{5,9},{9,5},{13,1},{2,14},{6,10},... | collective-permute-start | bytes 61448 | tf_op jit(solution)/shard_map/ppermute | solution.py:390
  6.3 0.0 collective-permute-start.1
  6.3 0.4 %collective-permute-start = (f32[5,8,128]{2,1,0:T(8,128)S(1)}, f32[5,8,128]{2,1,0:T(8,128)S(1)}, u32[]{:S(2)}, u32[]{:S(2)}) collective-permute-start(f32[5,8,128]{2,1,0:T(8,128)S(1)} %pack.1), channel_id=1, source_target_pairs={{0,4},{4,0},{8,12},{12,8},{1,5},{5,1},{9,13},{13,9},{2,6},{6,2},{1... | collective-permute-start | bytes 61448 | tf_op jit(solution)/shard_map/ppermute | solution.py:390
  6.6 1.0 %constant_dynamic-slice_fusion = (f32[6,16,480]{2,1,0:T(8,128)S(1)}, f32[6,16,480]{2,1,0:T(8,128)S(1)}) fusion(f32[24,64,480]{2,1,0:T(8,128)} %target_ref.1, s32[]{:T(128)S(6)} %select_n.12, s32[]{:T(128)S(6)} %select_n.11, s32[]{:T(128)S(6)} %select_n.10), kind=kLoop, calls=%fused_computation.2 | loop fusion | bytes 737292 | tf_op jit(solution)/shard_map/dynamic_slice | solution.py:377
  7.7 0.0 collective-permute-done.2
  7.7 2.1 %collective-permute-done.1 = f32[5,8,128]{2,1,0:T(8,128)S(1)} collective-permute-done((f32[5,8,128]{2,1,0:T(8,128)S(1)}, f32[5,8,128]{2,1,0:T(8,128)S(1)}, u32[]{:S(2)}, u32[]{:S(2)}) %collective-permute-start.1) | collective-permute-done | bytes 20512 | tf_op jit(solution)/shard_map/ppermute | solution.py:390
  9.8 0.0 collective-permute-done
  9.8 3.3 %collective-permute-start.6 = (f32[4,5,8,128]{3,2,1,0:T(8,128)S(1)}, f32[4,5,8,128]{3,2,1,0:T(8,128)S(1)}, u32[]{:S(2)}, u32[]{:S(2)}) collective-permute-start(f32[4,5,8,128]{3,2,1,0:T(8,128)S(1)} %pad_maximum_fusion.atoms_ref), channel_id=1, source_target_pairs={{1,2},{3,0},{2,1},{0,3},{5,6},{7,4},{6,5},{4,7},{9,10},{11,8},{10,... | collective-permute-start | bytes 245768 | tf_op jit(solution)/shard_map/ppermute | solution.py:382
  13.1 0.0 collective-permute-start.5
  13.1 0.5 %collective-permute-start.3 = (f32[6,16,480]{2,1,0:T(8,128)S(1)}, f32[6,16,480]{2,1,0:T(8,128)S(1)}, u32[]{:S(2)}, u32[]{:S(2)}) collective-permute-start(f32[6,16,480]{2,1,0:T(8,128)S(1)} %get-tuple-element.19), channel_id=1, source_target_pairs={{0,1},{2,3},{1,0},{3,2},{4,5},{6,7},{5,4},{7,6},{8,9},{10,11},{9,8... | collective-permute-start | bytes 552968 | tf_op jit(solution)/shard_map/ppermute | solution.py:382
  13.6 0.1 collective-permute-start.4
  13.7 2.6 %collective-permute-done.6.far_ref = f32[4,5,8,128]{3,2,1,0:T(8,128)S(1)} collective-permute-done((f32[4,5,8,128]{3,2,1,0:T(8,128)S(1)}, f32[4,5,8,128]{3,2,1,0:T(8,128)S(1)}, u32[]{:S(2)}, u32[]{:S(2)}) %collective-permute-start.6) | collective-permute-done | bytes 81952 | tf_op jit(solution)/shard_map/ppermute | solution.py:382
  16.4 0.0 collective-permute-done.5.near_ref
  16.4 5.9 %splat.1 = (f32[4,576,512]{2,1,0:T(8,128)S(1)}, f32[24,16,480]{2,1,0:T(8,128)S(1)}, bf16[32,512,128]{2,1,0:T(8,128)(2,1)S(1)}, bf16[32,512,128]{2,1,0:T(8,128)(2,1)S(1)}) custom-call(f32[4,5,8,128]{3,2,1,0:T(8,128)S(1)} %pad_maximum_fusion.atoms_ref, f32[4,5,8,128]{3,2,1,0:T(8,128)S(1)} %collective-permute-done.5.near_ref, ...), custom_call_target="tpu_custom_call" | custom-call | flops 6000000000 | bytes 14000000 | tf_op jit(solution)/shard_map/splat/pallas_call | solution.py:411
  22.3 0.0 collective-permute-done.3.near_target
  22.3 0.0 collective-permute-done.4.far_target
  22.3 5.2 %pull.1 = (f32[24,16,480]{2,1,0:T(8,128)}, f32[3,8,128]{2,1,0:T(8,128)S(1)}, f32[3,8,128]{2,1,0:T(8,128)S(1)}, f32[3,8,128]{2,1,0:T(8,128)S(1)}, f32[3,8,128]{2,1,0:T(8,128)S(1)}) custom-call(f32[4,5,8,128]{3,2,1,0:T(8,128)S(1)} %pad_maximum_fusion.atoms_ref, f32[6,16,480]{2,1,0:T(8,128)S(1)} %collective-permute-done.3.near_target, ...), custom_call_target="tpu_custom_call" | custom-call | flops 6000000000 | bytes 14000000 | tf_op jit(solution)/shard_map/pull/pallas_call | solution.py:432
  27.5 1.8 %collective-permute-start.7 = (f32[3,8,128]{2,1,0:T(8,128)S(1)}, f32[3,8,128]{2,1,0:T(8,128)S(1)}, u32[]{:S(2)}, u32[]{:S(2)}) collective-permute-start(f32[3,8,128]{2,1,0:T(8,128)S(1)} %get-tuple-element.27), channel_id=1, source_target_pairs={{0,8},{4,12},{8,0},{12,4},{1,9},{5,13},{9,1},{13,5},{2,10},{6,14},... | collective-permute-start | bytes 36872 | tf_op jit(solution)/shard_map/ppermute | solution.py:390
  29.3 0.0 collective-permute-start.8
  29.3 0.9 %collective-permute-start.9 = (f32[3,8,128]{2,1,0:T(8,128)S(1)}, f32[3,8,128]{2,1,0:T(8,128)S(1)}, u32[]{:S(2)}, u32[]{:S(2)}) collective-permute-start(f32[3,8,128]{2,1,0:T(8,128)S(1)} %get-tuple-element.29), channel_id=1, source_target_pairs={{0,4},{4,0},{8,12},{12,8},{1,5},{5,1},{9,13},{13,9},{2,6},{6,2},{1... | collective-permute-start | bytes 36872 | tf_op jit(solution)/shard_map/ppermute | solution.py:390
  30.2 0.8 %collective-permute-done.7 = f32[3,8,128]{2,1,0:T(8,128)S(1)} collective-permute-done((f32[3,8,128]{2,1,0:T(8,128)S(1)}, f32[3,8,128]{2,1,0:T(8,128)S(1)}, u32[]{:S(2)}, u32[]{:S(2)}) %collective-permute-start.7) | collective-permute-done | bytes 12320 | tf_op jit(solution)/shard_map/ppermute | solution.py:390
  31.0 2.6 %collective-permute-done.8 = f32[3,8,128]{2,1,0:T(8,128)S(1)} collective-permute-done((f32[3,8,128]{2,1,0:T(8,128)S(1)}, f32[3,8,128]{2,1,0:T(8,128)S(1)}, u32[]{:S(2)}, u32[]{:S(2)}) %collective-permute-start.8) | collective-permute-done | bytes 12320 | tf_op jit(solution)/shard_map/ppermute | solution.py:390
  33.7 0.0 collective-permute-done.9
  33.7 0.6 %add_add_fusion = f32[3,8,128]{2,1,0:T(8,128)} fusion(f32[3,8,128]{2,1,0:T(8,128)S(1)} %collective-permute-done.9, f32[3,8,128]{2,1,0:T(8,128)S(1)} %collective-permute-done.8, f32[3,8,128]{2,1,0:T(8,128)S(1)} %get-tuple-element.26, f32[3,8,128]{2,1,0:T(8,128)S(1)} %collective-permute-done.7), kind=kLoop, calls=%fused_computation.1 | loop fusion | flops 9216 | bytes 61440 | tf_op jit(solution)/shard_map/add | solution.py:455
  (1 shorter events, 0.0 us)
Async XLA Ops:
  2.0 5.6 %collective-permute-start.2 = (f32[5,8,128]{2,1,0:T(8,128)S(1)}, f32[5,8,128]{2,1,0:T(8,128)S(1)}, u32[]{:S(2)}, u32[]{:S(2)}) collective-permute-start(f32[5,8,128]{2,1,0:T(8,128)S(1)} %pack.1), channel_id=1, source_target_pairs={{0,12},{4,8},{8,4},{12,0},{1,13},{5,9},{9,5},{13,1},{2,14},{6,10},... | collective-permute-start | bytes 61448 | tf_op jit(solution)/shard_map/ppermute | solution.py:390
  6.3 3.5 %collective-permute-start.1 = (f32[5,8,128]{2,1,0:T(8,128)S(1)}, f32[5,8,128]{2,1,0:T(8,128)S(1)}, u32[]{:S(2)}, u32[]{:S(2)}) collective-permute-start(f32[5,8,128]{2,1,0:T(8,128)S(1)} %pack.1), channel_id=1, source_target_pairs={{0,8},{4,12},{8,0},{12,4},{1,9},{5,13},{9,1},{13,5},{2,10},{6,14},... | collective-permute-start | bytes 61448 | tf_op jit(solution)/shard_map/ppermute | solution.py:390
  6.3 3.5 %collective-permute-start = (f32[5,8,128]{2,1,0:T(8,128)S(1)}, f32[5,8,128]{2,1,0:T(8,128)S(1)}, u32[]{:S(2)}, u32[]{:S(2)}) collective-permute-start(f32[5,8,128]{2,1,0:T(8,128)S(1)} %pack.1), channel_id=1, source_target_pairs={{0,4},{4,0},{8,12},{12,8},{1,5},{5,1},{9,13},{13,9},{2,6},{6,2},{1... | collective-permute-start | bytes 61448 | tf_op jit(solution)/shard_map/ppermute | solution.py:390
  9.8 6.6 %collective-permute-start.6 = (f32[4,5,8,128]{3,2,1,0:T(8,128)S(1)}, f32[4,5,8,128]{3,2,1,0:T(8,128)S(1)}, u32[]{:S(2)}, u32[]{:S(2)}) collective-permute-start(f32[4,5,8,128]{3,2,1,0:T(8,128)S(1)} %pad_maximum_fusion.atoms_ref), channel_id=1, source_target_pairs={{1,2},{3,0},{2,1},{0,3},{5,6},{7,4},{6,5},{4,7},{9,10},{11,8},{10,... | collective-permute-start | bytes 245768 | tf_op jit(solution)/shard_map/ppermute | solution.py:382
  13.1 3.3 %collective-permute-start.5 = (f32[4,5,8,128]{3,2,1,0:T(8,128)S(1)}, f32[4,5,8,128]{3,2,1,0:T(8,128)S(1)}, u32[]{:S(2)}, u32[]{:S(2)}) collective-permute-start(f32[4,5,8,128]{3,2,1,0:T(8,128)S(1)} %pad_maximum_fusion.atoms_ref), channel_id=1, source_target_pairs={{0,1},{2,3},{1,0},{3,2},{4,5},{6,7},{5,4},{7,6},{8,9},{10,11},{9,8... | collective-permute-start | bytes 245768 | tf_op jit(solution)/shard_map/ppermute | solution.py:382
  13.1 9.2 %collective-permute-start.3 = (f32[6,16,480]{2,1,0:T(8,128)S(1)}, f32[6,16,480]{2,1,0:T(8,128)S(1)}, u32[]{:S(2)}, u32[]{:S(2)}) collective-permute-start(f32[6,16,480]{2,1,0:T(8,128)S(1)} %get-tuple-element.19), channel_id=1, source_target_pairs={{0,1},{2,3},{1,0},{3,2},{4,5},{6,7},{5,4},{7,6},{8,9},{10,11},{9,8... | collective-permute-start | bytes 552968 | tf_op jit(solution)/shard_map/ppermute | solution.py:382
  13.6 8.7 %collective-permute-start.4 = (f32[6,16,480]{2,1,0:T(8,128)S(1)}, f32[6,16,480]{2,1,0:T(8,128)S(1)}, u32[]{:S(2)}, u32[]{:S(2)}) collective-permute-start(f32[6,16,480]{2,1,0:T(8,128)S(1)} %get-tuple-element.20), channel_id=1, source_target_pairs={{1,2},{3,0},{2,1},{0,3},{5,6},{7,4},{6,5},{4,7},{9,10},{11,8},{10,... | collective-permute-start | bytes 552968 | tf_op jit(solution)/shard_map/ppermute | solution.py:382
  27.5 3.5 %collective-permute-start.7 = (f32[3,8,128]{2,1,0:T(8,128)S(1)}, f32[3,8,128]{2,1,0:T(8,128)S(1)}, u32[]{:S(2)}, u32[]{:S(2)}) collective-permute-start(f32[3,8,128]{2,1,0:T(8,128)S(1)} %get-tuple-element.27), channel_id=1, source_target_pairs={{0,8},{4,12},{8,0},{12,4},{1,9},{5,13},{9,1},{13,5},{2,10},{6,14},... | collective-permute-start | bytes 36872 | tf_op jit(solution)/shard_map/ppermute | solution.py:390
  29.3 4.3 %collective-permute-start.8 = (f32[3,8,128]{2,1,0:T(8,128)S(1)}, f32[3,8,128]{2,1,0:T(8,128)S(1)}, u32[]{:S(2)}, u32[]{:S(2)}) collective-permute-start(f32[3,8,128]{2,1,0:T(8,128)S(1)} %get-tuple-element.28), channel_id=1, source_target_pairs={{0,12},{4,8},{8,4},{12,0},{1,13},{5,9},{9,5},{13,1},{2,14},{6,10},... | collective-permute-start | bytes 36872 | tf_op jit(solution)/shard_map/ppermute | solution.py:390
  29.3 4.3 %collective-permute-start.9 = (f32[3,8,128]{2,1,0:T(8,128)S(1)}, f32[3,8,128]{2,1,0:T(8,128)S(1)}, u32[]{:S(2)}, u32[]{:S(2)}) collective-permute-start(f32[3,8,128]{2,1,0:T(8,128)S(1)} %get-tuple-element.29), channel_id=1, source_target_pairs={{0,4},{4,0},{8,12},{12,8},{1,5},{5,1},{9,13},{13,9},{2,6},{6,2},{1... | collective-permute-start | bytes 36872 | tf_op jit(solution)/shard_map/ppermute | solution.py:390
where the time goes:
time: 35 us; the launch traced here: 34.3 us
  Pallas kernels  11.9 us (34%)
  starting transfers between devices  11.2 us (32%)
  waiting for transfers between devices  8.18 us (23%)
  between operations  1.34 us (4%)
  local copies, waits for them, and re-layouts  1.05 us (3%)
  other arithmetic  0.61 us (2%)
    ppermute x6, starting transfers between devices, across(): return lax.ppermute(block, 'replica', [(i, i ^ k) for i in range(members)])  7.29 us
    pallas_call x1, Pallas kernels, shards(): pl.pallas_call(functools.partial(splat_kernel, members, zp, zs, sliced, s...  5.93 us
    ppermute x6, waiting for transfers between devices, across(): return lax.ppermute(block, 'replica', [(i, i ^ k) for i in range(members)])  5.53 us
    pallas_call x1, Pallas kernels, shards(): pl.pallas_call(functools.partial(pull_kernel, members, zp, zs, stash), ou...  5.18 us
    ppermute x4, starting transfers between devices, swap(): return lax.ppermute(block, 'sx', pairs + [(b, a) for a, b in pairs])  3.92 us
    ppermute x4, waiting for transfers between devices, swap(): return lax.ppermute(block, 'sx', pairs + [(b, a) for a, b in pairs])  2.65 us
    dynamic_slice x1, local copies, waits for them, and re-layouts, edge(): return lax.dynamic_slice(target, (plane, z_first, 0), (REACH, zp, NY))  1.05 us
    pallas_call x1, Pallas kernels, shards(): pl.pallas_call(pack_kernel, out_shape=jax.ShapeDtypeStruct((FIELDS,) + bl...  0.75 us
  transfers between devices with their start and end apart: 10, of which 4 were waited for; matrix products, arithmetic and copies ran while one was open for 3% of the time, Pallas kernels for 17%

commit v1 on v0

--- a/solution.py
+++ b/solution.py
@@ -20,7 +20,6 @@
 LANES = 512
 FIELDS = 5
 HALF_LOG2E = 0.5 * math.log2(math.e)
-STASH_LIMIT = 4
 
 noise_floor = 0.05
 
@@ -103,43 +102,48 @@
         table[:, NY:, :] = jnp.zeros((table.shape[0], LANES - NY, BLOCK), jnp.bfloat16)
 
 
-def splat_kernel(
-    members, zp, zs, sliced, stash, atoms_ref, near_ref, far_ref, target_ref, rho, wanted, *rest
-):
-    if stash:
-        gy, slope, gy_side, sides, more_list, side_list, sem = rest
+def splat_kernel(members, zp, zs, sliced, stash, stage, *refs):
+    slope = None
+    if stage == "own":
+        atoms_ref, rho, gy, slope, more_list = refs
+    elif stage == "side":
+        atoms_ref, near_ref, far_ref, target_ref, _, _, _, rho, gy, slope, *refs = refs
+        wanted, gy_side, sides, more_list, side_list, sem = refs
     else:
-        gy, gy_side, sides, more_list, side_list, sem = rest
-        slope = None
-    odd = lax.rem(lax.axis_index("sx"), 2)
-    if sliced:
-        z_first = pl.multiple_of(lax.axis_index("replica") * zs, 8)
-        source = target_ref.at[:, pl.ds(z_first, zs), :]
-    else:
-        source = target_ref
-    fetch = pltpu.make_async_copy(source, wanted, sem)
-    fetch.start()
-
+        atoms_ref, near_ref, far_ref, target_ref, rho, *refs = refs
+        wanted, gy, gy_side, sides, more_list, side_list, sem = refs
     brick = lax.axis_index("sx")
+    odd = lax.rem(brick, 2)
     inner = (brick > 0) & (brick < lax.axis_size("sx") - 1)
 
-    def list_member(member, counts):
-        own, near, far = (live_of(ref, member) for ref in (atoms_ref, near_ref, far_ref))
-        far = jnp.where(inner, far, 0)
+    if stage != "own":
+        if sliced:
+            z_first = pl.multiple_of(lax.axis_index("replica") * zs, 8)
+            source = target_ref.at[:, pl.ds(z_first, zs), :]
+        else:
+            source = target_ref
+        fetch = pltpu.make_async_copy(source, wanted, sem)
+        fetch.start()
+
+    def list_own(member, count):
+        return listed(more_list, count, 2, 2, member * BLOCKS, live_of(atoms_ref, member))
+
+    def list_sides(member, count):
         base = member * BLOCKS
         sides[member] = near_ref[member]
         sides[members + member] = far_ref[member]
-        side_count = listed(side_list, counts[1], 0, 1, base, near)
-        return (
-            listed(more_list, counts[0], 2, 2, base, own),
-            listed(side_list, side_count, 0, 1, members * BLOCKS + base, far),
-        )
-
-    more_count, side_count = lax.fori_loop(
-        0, members, list_member, (jnp.int32(0),) * 2, unroll=members <= 4
-    )
-    zero_tails(gy, gy_side)
-    if stash:
+        count = listed(side_list, count, 0, 1, base, live_of(near_ref, member))
+        far = jnp.where(inner, live_of(far_ref, member), 0)
+        return listed(side_list, count, 0, 1, members * BLOCKS + base, far)
+
+    unroll = members <= 4
+    more_count = lax.fori_loop(0, members, list_own, jnp.int32(0), unroll=unroll)
+    if stage != "own":
+        side_count = lax.fori_loop(0, members, list_sides, jnp.int32(0), unroll=unroll)
+        zero_tails(gy_side)
+    if stage != "side":
+        zero_tails(gy)
+    if stage == "own":
         zero_tails(slope)
     tables = Tables(zp, zs, atoms_ref)
 
@@ -176,12 +180,24 @@
         return carry
 
     start_group = min(members, 4)
-    lax.fori_loop(0, members // start_group, start_members, 0)
+    if stage != "side":
+        lax.fori_loop(0, members // start_group, start_members, 0)
 
     def more_pair(unit, part):
         code = more_list[unit]
         member, block = split(code)
         rho[member] += own_splat(member, block, part)
+
+    def two_pairs(step_at, carry):
+        more_pair(2 * step_at, 0)
+        more_pair(2 * step_at + 1, 1)
+        return carry
+
+    early = jnp.minimum(lax.shift_right_logical(more_count, 1), 1)
+    if stage == "own":
+        lax.fori_loop(0, early, two_pairs, 0)
+        return
+    past = 2 * early if stage == "side" else 0
 
     side_group = gy_side.shape[0]
 
@@ -208,12 +224,12 @@
             rho[member, at, :] += matmul_t(side_left, gy_side[part])
 
     def both(step_at, carry):
-        more_pair(step_at, 0)
+        more_pair(past + step_at, 0)
         side_units(step_at)
         return carry
 
     def more_alone(step_at, carry):
-        more_pair(step_at, 0)
+        more_pair(past + step_at, 0)
         return carry
 
     def side_alone(step_at, carry):
@@ -221,9 +237,9 @@
         return carry
 
     side_steps = (side_count + side_group - 1) // side_group
-    shared = jnp.minimum(more_count, side_steps)
+    shared = jnp.minimum(more_count - past, side_steps)
     lax.fori_loop(0, shared, both, 0)
-    lax.fori_loop(shared, more_count, more_alone, 0)
+    lax.fori_loop(shared, more_count - past, more_alone, 0)
     lax.fori_loop(shared, side_steps, side_alone, 0)
     fetch.wait()
 
@@ -344,7 +360,7 @@
     zp = max(zs, 8)
     sliced = zs % 8 == 0
     few = members <= 4 and members & (members - 1) == 0
-    stash = members <= STASH_LIMIT
+    stash = few
     blocks = (BLOCKS, BLOCK)
     vmem = pl.BlockSpec(memory_space=pltpu.VMEM)
     anywhere = pl.BlockSpec(memory_space=pl.ANY)
@@ -407,28 +423,53 @@
         else [jax.ShapeDtypeStruct((members, 3) + blocks, jnp.float32)]
     )
     table = ((members * BLOCKS if stash else 8), LANES, BLOCK)
-    tables = [jax.ShapeDtypeStruct(table, jnp.bfloat16)] * 2 if stash else []
-    splat = pl.pallas_call(
-        functools.partial(splat_kernel, members, zp, zs, sliced, stash),
-        out_shape=[
-            jax.ShapeDtypeStruct((members, SPAN * zp, LANES), jnp.float32),
-            jax.ShapeDtypeStruct((CX, zp, NY), jnp.float32),
-        ]
-        + tables,
-        in_specs=[vmem] * 3 + [hbm],
-        out_specs=[vmem] * (2 + len(tables)),
-        scratch_shapes=([] if stash else [pltpu.VMEM(table, jnp.bfloat16)])
-        + [
-            pltpu.VMEM((4, LANES, BLOCK), jnp.bfloat16),
-            pltpu.VMEM((2 * members, FIELDS) + blocks, jnp.float32),
-            pltpu.SMEM((members * BLOCKS + 1,), jnp.int32),
-            pltpu.SMEM((2 * members * BLOCKS + 1,), jnp.int32),
-            pltpu.SemaphoreType.DMA,
-        ],
-        compiler_params=pltpu.CompilerParams(vmem_limit_bytes=24 * 1024 * 1024),
-        cost_estimate=pl.CostEstimate(flops=6_000_000_000, bytes_accessed=14_000_000, transcendentals=0),
-        name="splat",
-    )(everyone, near, far, pltpu.with_memory_space_constraint(target, pltpu.HBM))
+    kept = [((members, SPAN * zp, LANES), jnp.float32)] + [(table, jnp.bfloat16)] * (2 if stash else 0)
+    goal = jax.ShapeDtypeStruct((CX, zp, NY), jnp.float32)
+    lists = [pltpu.SMEM((n * members * BLOCKS + 1,), jnp.int32) for n in (1, 2)]
+    work = [
+        pltpu.VMEM((4, LANES, BLOCK), jnp.bfloat16),
+        pltpu.VMEM((2 * members, FIELDS) + blocks, jnp.float32),
+        *lists,
+        pltpu.SemaphoreType.DMA,
+    ]
+    params = pltpu.CompilerParams(vmem_limit_bytes=24 * 1024 * 1024)
+    goal_source = pltpu.with_memory_space_constraint(target, pltpu.HBM)
+    if few:
+        kept = [pltpu.VMEM(*k) for k in kept]
+        first = pl.pallas_call(
+            functools.partial(splat_kernel, members, zp, zs, sliced, stash, "own"),
+            out_shape=kept,
+            in_specs=[vmem],
+            out_specs=[vmem] * 3,
+            scratch_shapes=lists[:1],
+            compiler_params=params,
+            cost_estimate=pl.CostEstimate(flops=2_000_000_000, bytes_accessed=1_000_000, transcendentals=0),
+            name="splat_own",
+        )(everyone)
+        first = [pltpu.with_memory_space_constraint(x, pltpu.VMEM) for x in first]
+        *splat, wanted = pl.pallas_call(
+            functools.partial(splat_kernel, members, zp, zs, sliced, stash, "side"),
+            out_shape=kept + [goal],
+            in_specs=[vmem] * 3 + [hbm] + [vmem] * 3,
+            out_specs=[vmem] * 4,
+            scratch_shapes=work,
+            input_output_aliases={4: 0, 5: 1, 6: 2},
+            compiler_params=params,
+            cost_estimate=pl.CostEstimate(flops=500_000_000, bytes_accessed=1_000_000, transcendentals=0),
+            name="splat_side",
+        )(everyone, near, far, goal_source, *first)
+        splat.insert(1, wanted)
+    else:
+        splat = pl.pallas_call(
+            functools.partial(splat_kernel, members, zp, zs, sliced, stash, "all"),
+            out_shape=[jax.ShapeDtypeStruct(*kept[0]), goal],
+            in_specs=[vmem] * 3 + [hbm],
+            out_specs=[vmem] * 2,
+            scratch_shapes=[pltpu.VMEM(table, jnp.bfloat16)] + work,
+            compiler_params=params,
+            cost_estimate=pl.CostEstimate(flops=6_000_000_000, bytes_accessed=14_000_000, transcendentals=0),
+            name="splat",
+        )(everyone, near, far, goal_source)
     mean, *partial = pl.pallas_call(
         functools.partial(pull_kernel, members, zp, zs, stash),
         out_shape=[jax.ShapeDtypeStruct((CX, zp, NY), jnp.float32)] + force_shapes,

time: 35 us -> 33 us (0.943)
  the two profiles are of different devices: /device:TPU:1 before, /device:TPU:0 now
where the time goes in v1:
time: 33 us; the launch traced here: 32.5 us
  starting transfers between devices  11.6 us (35%)
  waiting for transfers between devices  9.65 us (29%)
  Pallas kernels  8.24 us (25%)
  between operations  1.34 us (4%)
  local copies, waits for them, and re-layouts  1.05 us (3%)
  other arithmetic  0.61 us (2%)
    ppermute x6, starting transfers between devices, across(): return lax.ppermute(block, 'replica', [(i, i ^ k) for i in range(members)])  9.31 us
    ppermute x6, waiting for transfers between devices, across(): return lax.ppermute(block, 'replica', [(i, i ^ k) for i in range(members)])  7.01 us
    pallas_call x1, Pallas kernels, shards(): pl.pallas_call(functools.partial(pull_kernel, members, zp, zs, stash), ou...  4.06 us
    pallas_call x2, Pallas kernels, shards(): pl.pallas_call(functools.partial(splat_kernel, members, zp, zs, sliced, s...  3.43 us
    ppermute x4, waiting for transfers between devices, swap(): return lax.ppermute(block, 'sx', pairs + [(b, a) for a, b in pairs])  2.64 us
    ppermute x4, starting transfers between devices, swap(): return lax.ppermute(block, 'sx', pairs + [(b, a) for a, b in pairs])  2.31 us
    dynamic_slice x1, local copies, waits for them, and re-layouts, edge(): return lax.dynamic_slice(target, (plane, z_first, 0), (REACH, zp, NY))  1.05 us
    pallas_call x1, Pallas kernels, shards(): pl.pallas_call(pack_kernel, out_shape=jax.ShapeDtypeStruct((FIELDS,) + bl...  0.75 us
  transfers between devices with their start and end apart: 10, of which 6 were waited for; matrix products, arithmetic and copies ran while one was open for 3% of the time, Pallas kernels for 11%

profile of v1, /device:TPU:0, one launch (start us, length us, event | category | flops | bytes accessed | tf_op | source)
XLA Modules:
  0.0 32.5 jit_solution(3162638896592172469)
XLA Ops:
  1.3 0.7 %pack.1 = f32[5,8,128]{2,1,0:T(8,128)S(1)} custom-call(f32[3,8,128]{2,1,0:T(8,128)} %bitcast.12, f32[8,128]{1,0:T(8,128)} %bitcast.14, f32[8,128]{1,0:T(8,128)} %bitcast.15, s32[1,1]{1,0:T(1,128)S(6)} %copy.15.live_ref), custom_call_target="tpu_custom_call" | custom-call | tf_op jit(solution)/shard_map/pack/pallas_call | solution.py:373
  2.0 5.1 %collective-permute-start.2 = (f32[5,8,128]{2,1,0:T(8,128)S(1)}, f32[5,8,128]{2,1,0:T(8,128)S(1)}, u32[]{:S(2)}, u32[]{:S(2)}) collective-permute-start(f32[5,8,128]{2,1,0:T(8,128)S(1)} %pack.1), channel_id=1, source_target_pairs={{0,12},{4,8},{8,4},{12,0},{1,13},{5,9},{9,5},{13,1},{2,14},{6,10},... | collective-permute-start | bytes 61448 | tf_op jit(solution)/shard_map/ppermute | solution.py:406
  7.1 0.0 collective-permute-start.1
  7.2 0.6 %collective-permute-start = (f32[5,8,128]{2,1,0:T(8,128)S(1)}, f32[5,8,128]{2,1,0:T(8,128)S(1)}, u32[]{:S(2)}, u32[]{:S(2)}) collective-permute-start(f32[5,8,128]{2,1,0:T(8,128)S(1)} %pack.1), channel_id=1, source_target_pairs={{0,4},{4,0},{8,12},{12,8},{1,5},{5,1},{9,13},{13,9},{2,6},{6,2},{1... | collective-permute-start | bytes 61448 | tf_op jit(solution)/shard_map/ppermute | solution.py:406
  7.8 1.0 %constant_dynamic-slice_fusion = (f32[6,16,480]{2,1,0:T(8,128)S(1)}, f32[6,16,480]{2,1,0:T(8,128)S(1)}) fusion(f32[24,64,480]{2,1,0:T(8,128)} %refs_3_.1, s32[]{:T(128)S(6)} %select_n.12, s32[]{:T(128)S(6)} %select_n.11, s32[]{:T(128)S(6)} %select_n.10), kind=kLoop, calls=%fused_computation.2 | loop fusion | bytes 737292 | tf_op jit(solution)/shard_map/dynamic_slice | solution.py:393
  8.8 0.1 collective-permute-done.2
  8.9 2.9 %collective-permute-done.1 = f32[5,8,128]{2,1,0:T(8,128)S(1)} collective-permute-done((f32[5,8,128]{2,1,0:T(8,128)S(1)}, f32[5,8,128]{2,1,0:T(8,128)S(1)}, u32[]{:S(2)}, u32[]{:S(2)}) %collective-permute-start.1) | collective-permute-done | bytes 20512 | tf_op jit(solution)/shard_map/ppermute | solution.py:406
  11.8 0.0 collective-permute-done
  11.8 0.1 collective-permute-start.6
  11.9 1.6 %collective-permute-start.5 = (f32[4,5,8,128]{3,2,1,0:T(8,128)S(1)}, f32[4,5,8,128]{3,2,1,0:T(8,128)S(1)}, u32[]{:S(2)}, u32[]{:S(2)}) collective-permute-start(f32[4,5,8,128]{3,2,1,0:T(8,128)S(1)} %pad_maximum_fusion.refs_0_.atoms_ref), channel_id=1, source_target_pairs={{0,1},{2,3},{1,0},{3,2},{4,5},{6,7},{5,4},{7,6},{8,9},{10,11},{9,8... | collective-permute-start | bytes 245768 | tf_op jit(solution)/shard_map/ppermute | solution.py:398
  13.5 0.0 collective-permute-start.3
  13.5 0.6 %collective-permute-start.4 = (f32[6,16,480]{2,1,0:T(8,128)S(1)}, f32[6,16,480]{2,1,0:T(8,128)S(1)}, u32[]{:S(2)}, u32[]{:S(2)}) collective-permute-start(f32[6,16,480]{2,1,0:T(8,128)S(1)} %get-tuple-element.23), channel_id=1, source_target_pairs={{1,2},{3,0},{2,1},{0,3},{5,6},{7,4},{6,5},{4,7},{9,10},{11,8},{10,... | collective-permute-start | bytes 552968 | tf_op jit(solution)/shard_map/ppermute | solution.py:398
  14.2 2.0 %splat_own.1 = (f32[4,576,512]{2,1,0:T(8,128)S(1)}, bf16[32,512,128]{2,1,0:T(8,128)(2,1)S(1)}, bf16[32,512,128]{2,1,0:T(8,128)(2,1)S(1)}) custom-call(f32[4,5,8,128]{3,2,1,0:T(8,128)S(1)} %pad_maximum_fusion.refs_0_.atoms_ref), custom_call_target="tpu_custom_call" | custom-call | flops 2000000000 | bytes 1000000 | tf_op jit(solution)/shard_map/splat_own/pallas_call | solution.py:439
  16.1 0.5 %collective-permute-done.6.refs_2_ = f32[4,5,8,128]{3,2,1,0:T(8,128)S(1)} collective-permute-done((f32[4,5,8,128]{3,2,1,0:T(8,128)S(1)}, f32[4,5,8,128]{3,2,1,0:T(8,128)S(1)}, u32[]{:S(2)}, u32[]{:S(2)}) %collective-permute-start.6) | collective-permute-done | bytes 81952 | tf_op jit(solution)/shard_map/ppermute | solution.py:398
  16.6 0.0 collective-permute-done.5.refs_1_
  16.6 1.5 %splat_side.1 = (f32[4,576,512]{2,1,0:T(8,128)S(1)}, bf16[32,512,128]{2,1,0:T(8,128)(2,1)S(1)}, bf16[32,512,128]{2,1,0:T(8,128)(2,1)S(1)}, f32[24,16,480]{2,1,0:T(8,128)S(1)}) custom-call(f32[4,5,8,128]{3,2,1,0:T(8,128)S(1)} %pad_maximum_fusion.refs_0_.atoms_ref, ...), custom_call_target="tpu_custom_call", output_to_operand_aliasing={{0}: (4, {}), {1}: (5, {}), {2}: (6, {})} | custom-call | flops 500000000 | bytes 1000000 | tf_op jit(solution)/shard_map/splat_side/pallas_call | solution.py:450
  18.1 0.0 collective-permute-done.3.near_target
  18.1 2.2 %collective-permute-done.4.far_target = f32[6,16,480]{2,1,0:T(8,128)S(1)} collective-permute-done((f32[6,16,480]{2,1,0:T(8,128)S(1)}, f32[6,16,480]{2,1,0:T(8,128)S(1)}, u32[]{:S(2)}, u32[]{:S(2)}) %collective-permute-start.4) | collective-permute-done | bytes 184352 | tf_op jit(solution)/shard_map/ppermute | solution.py:398
  20.3 4.1 %pull.1 = (f32[24,16,480]{2,1,0:T(8,128)}, f32[3,8,128]{2,1,0:T(8,128)S(1)}, f32[3,8,128]{2,1,0:T(8,128)S(1)}, f32[3,8,128]{2,1,0:T(8,128)S(1)}, f32[3,8,128]{2,1,0:T(8,128)S(1)}) custom-call(f32[4,5,8,128]{3,2,1,0:T(8,128)S(1)} %pad_maximum_fusion.refs_0_.atoms_ref, f32[6,16,480]{2,1,0:T(8,128)S(1)} %collective-permute-done.3.near_target, ...), custom_call_target="tpu_custom_call" | custom-call | flops 6000000000 | bytes 14000000 | tf_op jit(solution)/shard_map/pull/pallas_call | solution.py:473
  24.3 2.1 %collective-permute-start.7 = (f32[3,8,128]{2,1,0:T(8,128)S(1)}, f32[3,8,128]{2,1,0:T(8,128)S(1)}, u32[]{:S(2)}, u32[]{:S(2)}) collective-permute-start(f32[3,8,128]{2,1,0:T(8,128)S(1)} %get-tuple-element.33), channel_id=1, source_target_pairs={{0,8},{4,12},{8,0},{12,4},{1,9},{5,13},{9,1},{13,5},{2,10},{6,14},... | collective-permute-start | bytes 36872 | tf_op jit(solution)/shard_map/ppermute | solution.py:406
  26.4 0.0 collective-permute-start.8
  26.5 1.4 %collective-permute-start.9 = (f32[3,8,128]{2,1,0:T(8,128)S(1)}, f32[3,8,128]{2,1,0:T(8,128)S(1)}, u32[]{:S(2)}, u32[]{:S(2)}) collective-permute-start(f32[3,8,128]{2,1,0:T(8,128)S(1)} %get-tuple-element.35), channel_id=1, source_target_pairs={{0,4},{4,0},{8,12},{12,8},{1,5},{5,1},{9,13},{13,9},{2,6},{6,2},{1... | collective-permute-start | bytes 36872 | tf_op jit(solution)/shard_map/ppermute | solution.py:406
  27.9 1.1 %collective-permute-done.7 = f32[3,8,128]{2,1,0:T(8,128)S(1)} collective-permute-done((f32[3,8,128]{2,1,0:T(8,128)S(1)}, f32[3,8,128]{2,1,0:T(8,128)S(1)}, u32[]{:S(2)}, u32[]{:S(2)}) %collective-permute-start.7) | collective-permute-done | bytes 12320 | tf_op jit(solution)/shard_map/ppermute | solution.py:406
  29.0 2.9 %collective-permute-done.8 = f32[3,8,128]{2,1,0:T(8,128)S(1)} collective-permute-done((f32[3,8,128]{2,1,0:T(8,128)S(1)}, f32[3,8,128]{2,1,0:T(8,128)S(1)}, u32[]{:S(2)}, u32[]{:S(2)}) %collective-permute-start.8) | collective-permute-done | bytes 12320 | tf_op jit(solution)/shard_map/ppermute | solution.py:406
  31.9 0.0 collective-permute-done.9
  31.9 0.6 %add_add_fusion = f32[3,8,128]{2,1,0:T(8,128)} fusion(f32[3,8,128]{2,1,0:T(8,128)S(1)} %collective-permute-done.9, f32[3,8,128]{2,1,0:T(8,128)S(1)} %collective-permute-done.8, f32[3,8,128]{2,1,0:T(8,128)S(1)} %get-tuple-element.32, f32[3,8,128]{2,1,0:T(8,128)S(1)} %collective-permute-done.7), kind=kLoop, calls=%fused_computation.1 | loop fusion | flops 9216 | bytes 61440 | tf_op jit(solution)/shard_map/add | solution.py:496
  (1 shorter events, 0.0 us)
Async XLA Ops:
  2.0 6.9 %collective-permute-start.2 = (f32[5,8,128]{2,1,0:T(8,128)S(1)}, f32[5,8,128]{2,1,0:T(8,128)S(1)}, u32[]{:S(2)}, u32[]{:S(2)}) collective-permute-start(f32[5,8,128]{2,1,0:T(8,128)S(1)} %pack.1), channel_id=1, source_target_pairs={{0,12},{4,8},{8,4},{12,0},{1,13},{5,9},{9,5},{13,1},{2,14},{6,10},... | collective-permute-start | bytes 61448 | tf_op jit(solution)/shard_map/ppermute | solution.py:406
  7.1 4.7 %collective-permute-start.1 = (f32[5,8,128]{2,1,0:T(8,128)S(1)}, f32[5,8,128]{2,1,0:T(8,128)S(1)}, u32[]{:S(2)}, u32[]{:S(2)}) collective-permute-start(f32[5,8,128]{2,1,0:T(8,128)S(1)} %pack.1), channel_id=1, source_target_pairs={{0,8},{4,12},{8,0},{12,4},{1,9},{5,13},{9,1},{13,5},{2,10},{6,14},... | collective-permute-start | bytes 61448 | tf_op jit(solution)/shard_map/ppermute | solution.py:406
  7.2 4.7 %collective-permute-start = (f32[5,8,128]{2,1,0:T(8,128)S(1)}, f32[5,8,128]{2,1,0:T(8,128)S(1)}, u32[]{:S(2)}, u32[]{:S(2)}) collective-permute-start(f32[5,8,128]{2,1,0:T(8,128)S(1)} %pack.1), channel_id=1, source_target_pairs={{0,4},{4,0},{8,12},{12,8},{1,5},{5,1},{9,13},{13,9},{2,6},{6,2},{1... | collective-permute-start | bytes 61448 | tf_op jit(solution)/shard_map/ppermute | solution.py:406
  11.8 4.8 %collective-permute-start.6 = (f32[4,5,8,128]{3,2,1,0:T(8,128)S(1)}, f32[4,5,8,128]{3,2,1,0:T(8,128)S(1)}, u32[]{:S(2)}, u32[]{:S(2)}) collective-permute-start(f32[4,5,8,128]{3,2,1,0:T(8,128)S(1)} %pad_maximum_fusion.refs_0_.atoms_ref), channel_id=1, source_target_pairs={{1,2},{3,0},{2,1},{0,3},{5,6},{7,4},{6,5},{4,7},{9,10},{11,8},{10,... | collective-permute-start | bytes 245768 | tf_op jit(solution)/shard_map/ppermute | solution.py:398
  11.9 4.7 %collective-permute-start.5 = (f32[4,5,8,128]{3,2,1,0:T(8,128)S(1)}, f32[4,5,8,128]{3,2,1,0:T(8,128)S(1)}, u32[]{:S(2)}, u32[]{:S(2)}) collective-permute-start(f32[4,5,8,128]{3,2,1,0:T(8,128)S(1)} %pad_maximum_fusion.refs_0_.atoms_ref), channel_id=1, source_target_pairs={{0,1},{2,3},{1,0},{3,2},{4,5},{6,7},{5,4},{7,6},{8,9},{10,11},{9,8... | collective-permute-start | bytes 245768 | tf_op jit(solution)/shard_map/ppermute | solution.py:398
  13.5 4.6 %collective-permute-start.3 = (f32[6,16,480]{2,1,0:T(8,128)S(1)}, f32[6,16,480]{2,1,0:T(8,128)S(1)}, u32[]{:S(2)}, u32[]{:S(2)}) collective-permute-start(f32[6,16,480]{2,1,0:T(8,128)S(1)} %get-tuple-element.22), channel_id=1, source_target_pairs={{0,1},{2,3},{1,0},{3,2},{4,5},{6,7},{5,4},{7,6},{8,9},{10,11},{9,8... | collective-permute-start | bytes 552968 | tf_op jit(solution)/shard_map/ppermute | solution.py:398
  13.5 6.7 %collective-permute-start.4 = (f32[6,16,480]{2,1,0:T(8,128)S(1)}, f32[6,16,480]{2,1,0:T(8,128)S(1)}, u32[]{:S(2)}, u32[]{:S(2)}) collective-permute-start(f32[6,16,480]{2,1,0:T(8,128)S(1)} %get-tuple-element.23), channel_id=1, source_target_pairs={{1,2},{3,0},{2,1},{0,3},{5,6},{7,4},{6,5},{4,7},{9,10},{11,8},{10,... | collective-permute-start | bytes 552968 | tf_op jit(solution)/shard_map/ppermute | solution.py:398
  24.3 4.7 %collective-permute-start.7 = (f32[3,8,128]{2,1,0:T(8,128)S(1)}, f32[3,8,128]{2,1,0:T(8,128)S(1)}, u32[]{:S(2)}, u32[]{:S(2)}) collective-permute-start(f32[3,8,128]{2,1,0:T(8,128)S(1)} %get-tuple-element.33), channel_id=1, source_target_pairs={{0,8},{4,12},{8,0},{12,4},{1,9},{5,13},{9,1},{13,5},{2,10},{6,14},... | collective-permute-start | bytes 36872 | tf_op jit(solution)/shard_map/ppermute | solution.py:406
  26.4 5.5 %collective-permute-start.8 = (f32[3,8,128]{2,1,0:T(8,128)S(1)}, f32[3,8,128]{2,1,0:T(8,128)S(1)}, u32[]{:S(2)}, u32[]{:S(2)}) collective-permute-start(f32[3,8,128]{2,1,0:T(8,128)S(1)} %get-tuple-element.34), channel_id=1, source_target_pairs={{0,12},{4,8},{8,4},{12,0},{1,13},{5,9},{9,5},{13,1},{2,14},{6,10},... | collective-permute-start | bytes 36872 | tf_op jit(solution)/shard_map/ppermute | solution.py:406
  26.5 5.4 %collective-permute-start.9 = (f32[3,8,128]{2,1,0:T(8,128)S(1)}, f32[3,8,128]{2,1,0:T(8,128)S(1)}, u32[]{:S(2)}, u32[]{:S(2)}) collective-permute-start(f32[3,8,128]{2,1,0:T(8,128)S(1)} %get-tuple-element.35), channel_id=1, source_target_pairs={{0,4},{4,0},{8,12},{12,8},{1,5},{5,1},{9,13},{13,9},{2,6},{6,2},{1... | collective-permute-start | bytes 36872 | tf_op jit(solution)/shard_map/ppermute | solution.py:406

commit v2 on v1

--- a/solution.py
+++ b/solution.py
@@ -275,7 +275,7 @@
         noise = noise_floor + spread * (1.0 / members)
         guess = pl.reciprocal(noise, approx=True)
         inv = guess * (2.0 - noise * guess)
-        pull = (goal[planes].reshape(group * zp, NY) - mean) * inv
+        pull = (goal[planes].astype(jnp.float32).reshape(group * zp, NY) - mean) * inv
         gain = (inv - pull * pull) * (1.0 / (members * members))
         offset = pull * (-1.0 / members) - gain * mean
         for m in range(members):
@@ -390,7 +390,8 @@
 
     def edge(plane):
         z_first = rank * zs if sliced else 0
-        return lax.dynamic_slice(target, (plane, z_first, 0), (REACH, zp, NY))
+        block = lax.dynamic_slice(target, (plane, z_first, 0), (REACH, zp, NY))
+        return block.astype(jnp.bfloat16)
 
     near_edge, far_edge = edge((CX - REACH) * (1 - odd)), edge((CX - REACH) * odd)
 

time: 33 us -> 32.6 us (0.988); the launches traced: 32.5 us -> 32.9 us
  Pallas kernels: 8.24 us -> 10.8 us
  waiting for transfers between devices: 9.65 us -> 7.49 us
    ppermute x4, waiting for transfers between devices: 2.64 us -> 0.47 us  [swap(): return lax.ppermute(block, 'sx', pairs + [(b, a) for a, b in pairs])]
    pallas_call x2, Pallas kernels: 3.43 us -> 4.83 us  [shards(): pl.pallas_call(functools.partial(splat_kernel, members, zp, zs, sliced, s...]
    pallas_call x1, Pallas kernels: 4.06 us -> 5.21 us  [shards(): pl.pallas_call(functools.partial(pull_kernel, members, zp, zs, stash), ou...]
    dynamic_slice x1 -> x0, local copies, waits for them, and re-layouts: 1.05 us -> none  [edge(): return lax.dynamic_slice(target, (plane, z_first, 0), (REACH, zp, NY))]
    convert_element_type x0 -> x1, local copies, waits for them, and re-layouts: none -> 1.05 us  [edge(): return block.astype(jnp.bfloat16)]
  transfers between devices with their start and end apart: 10 -> 10, of which waited for: 6 -> 5; matrix products, arithmetic and copies ran while one was open for 3% -> 3% of each run, Pallas kernels for 11% -> 15%
where the time goes in v2:
time: 32.6 us; the launch traced here: 32.9 us
  starting transfers between devices  11.6 us (36%)
  Pallas kernels  10.8 us (33%)
  waiting for transfers between devices  7.49 us (23%)
  between operations  1.35 us (4%)
  local copies, waits for them, and re-layouts  1.05 us (3%)
  other arithmetic  0.61 us (2%)
    ppermute x6, starting transfers between devices, across(): return lax.ppermute(block, 'replica', [(i, i ^ k) for i in range(members)])  9.31 us
    ppermute x6, waiting for transfers between devices, across(): return lax.ppermute(block, 'replica', [(i, i ^ k) for i in range(members)])  7.02 us
    pallas_call x1, Pallas kernels, shards(): pl.pallas_call(functools.partial(pull_kernel, members, zp, zs, stash), ou...  5.21 us
    pallas_call x2, Pallas kernels, shards(): pl.pallas_call(functools.partial(splat_kernel, members, zp, zs, sliced, s...  4.83 us
    ppermute x4, starting transfers between devices, swap(): return lax.ppermute(block, 'sx', pairs + [(b, a) for a, b in pairs])  2.31 us
    convert_element_type x1, local copies, waits for them, and re-layouts, edge(): return block.astype(jnp.bfloat16)  1.05 us
    pallas_call x1, Pallas kernels, shards(): pl.pallas_call(pack_kernel, out_shape=jax.ShapeDtypeStruct((FIELDS,) + bl...  0.75 us
  transfers between devices with their start and end apart: 10, of which 5 were waited for; matrix products, arithmetic and copies ran while one was open for 3% of the time, Pallas kernels for 15%

profile of v2, /device:TPU:0, one launch (start us, length us, event | category | flops | bytes accessed | tf_op | source)
XLA Modules:
  0.0 32.9 jit_solution(17348096305799094452)
XLA Ops:
  1.3 0.7 %pack.1 = f32[5,8,128]{2,1,0:T(8,128)S(1)} custom-call(f32[3,8,128]{2,1,0:T(8,128)} %bitcast.12, f32[8,128]{1,0:T(8,128)} %bitcast.14, f32[8,128]{1,0:T(8,128)} %bitcast.15, s32[1,1]{1,0:T(1,128)S(6)} %copy.15.live_ref), custom_call_target="tpu_custom_call" | custom-call | tf_op jit(solution)/shard_map/pack/pallas_call | solution.py:373
  2.0 5.1 %collective-permute-start.2 = (f32[5,8,128]{2,1,0:T(8,128)S(1)}, f32[5,8,128]{2,1,0:T(8,128)S(1)}, u32[]{:S(2)}, u32[]{:S(2)}) collective-permute-start(f32[5,8,128]{2,1,0:T(8,128)S(1)} %pack.1), channel_id=1, source_target_pairs={{0,12},{4,8},{8,4},{12,0},{1,13},{5,9},{9,5},{13,1},{2,14},{6,10},... | collective-permute-start | bytes 61448 | tf_op jit(solution)/shard_map/ppermute | solution.py:407
  7.1 0.0 collective-permute-start.1
  7.2 0.6 %collective-permute-start = (f32[5,8,128]{2,1,0:T(8,128)S(1)}, f32[5,8,128]{2,1,0:T(8,128)S(1)}, u32[]{:S(2)}, u32[]{:S(2)}) collective-permute-start(f32[5,8,128]{2,1,0:T(8,128)S(1)} %pack.1), channel_id=1, source_target_pairs={{0,4},{4,0},{8,12},{12,8},{1,5},{5,1},{9,13},{13,9},{2,6},{6,2},{1... | collective-permute-start | bytes 61448 | tf_op jit(solution)/shard_map/ppermute | solution.py:407
  7.8 1.0 %dynamic-slice_convert_fusion = (bf16[6,16,480]{2,1,0:T(8,128)(2,1)S(1)}, bf16[6,16,480]{2,1,0:T(8,128)(2,1)S(1)}) fusion(f32[24,64,480]{2,1,0:T(8,128)} %refs_3_.1, s32[]{:T(128)S(6)} %select_n.12, s32[]{:T(128)S(6)} %select_n.11, s32[]{:T(128)S(6)} %select_n.10), kind=kLoop, calls=%fused_computation | loop fusion | bytes 368652 | tf_op jit(solution)/shard_map/convert_element_type | solution.py:394
  8.8 0.1 collective-permute-done.2
  8.9 2.9 %collective-permute-done.1 = f32[5,8,128]{2,1,0:T(8,128)S(1)} collective-permute-done((f32[5,8,128]{2,1,0:T(8,128)S(1)}, f32[5,8,128]{2,1,0:T(8,128)S(1)}, u32[]{:S(2)}, u32[]{:S(2)}) %collective-permute-start.1) | collective-permute-done | bytes 20512 | tf_op jit(solution)/shard_map/ppermute | solution.py:407
  11.8 0.0 collective-permute-done
  11.8 0.1 collective-permute-start.6
  11.9 1.6 %collective-permute-start.5 = (f32[4,5,8,128]{3,2,1,0:T(8,128)S(1)}, f32[4,5,8,128]{3,2,1,0:T(8,128)S(1)}, u32[]{:S(2)}, u32[]{:S(2)}) collective-permute-start(f32[4,5,8,128]{3,2,1,0:T(8,128)S(1)} %pad_maximum_fusion.refs_0_.atoms_ref), channel_id=1, source_target_pairs={{0,1},{2,3},{1,0},{3,2},{4,5},{6,7},{5,4},{7,6},{8,9},{10,11},{9,8... | collective-permute-start | bytes 245768 | tf_op jit(solution)/shard_map/ppermute | solution.py:399
  13.5 0.0 collective-permute-start.3
  13.5 0.6 %collective-permute-start.4 = (bf16[6,16,480]{2,1,0:T(8,128)(2,1)S(1)}, bf16[6,16,480]{2,1,0:T(8,128)(2,1)S(1)}, u32[]{:S(2)}, u32[]{:S(2)}) collective-permute-start(bf16[6,16,480]{2,1,0:T(8,128)(2,1)S(1)} %get-tuple-element.23), channel_id=1, source_target_pairs={{1,2},{3,0},{2,1},{0,3},{5,6},{7,4},{6,5},{4,7},{9,10},{11,8},{10,... | collective-permute-start | bytes 276488 | tf_op jit(solution)/shard_map/ppermute | solution.py:399
  14.2 2.0 %splat_own.1 = (f32[4,576,512]{2,1,0:T(8,128)S(1)}, bf16[32,512,128]{2,1,0:T(8,128)(2,1)S(1)}, bf16[32,512,128]{2,1,0:T(8,128)(2,1)S(1)}) custom-call(f32[4,5,8,128]{3,2,1,0:T(8,128)S(1)} %pad_maximum_fusion.refs_0_.atoms_ref), custom_call_target="tpu_custom_call" | custom-call | flops 2000000000 | bytes 1000000 | tf_op jit(solution)/shard_map/splat_own/pallas_call | solution.py:440
  16.1 0.5 %collective-permute-done.6.refs_2_ = f32[4,5,8,128]{3,2,1,0:T(8,128)S(1)} collective-permute-done((f32[4,5,8,128]{3,2,1,0:T(8,128)S(1)}, f32[4,5,8,128]{3,2,1,0:T(8,128)S(1)}, u32[]{:S(2)}, u32[]{:S(2)}) %collective-permute-start.6) | collective-permute-done | bytes 81952 | tf_op jit(solution)/shard_map/ppermute | solution.py:399
  16.6 0.0 collective-permute-done.5.refs_1_
  16.6 2.9 %splat_side.1 = (f32[4,576,512]{2,1,0:T(8,128)S(1)}, bf16[32,512,128]{2,1,0:T(8,128)(2,1)S(1)}, bf16[32,512,128]{2,1,0:T(8,128)(2,1)S(1)}, f32[24,16,480]{2,1,0:T(8,128)S(1)}) custom-call(f32[4,5,8,128]{3,2,1,0:T(8,128)S(1)} %pad_maximum_fusion.refs_0_.atoms_ref, ...), custom_call_target="tpu_custom_call", output_to_operand_aliasing={{0}: (4, {}), {1}: (5, {}), {2}: (6, {})} | custom-call | flops 500000000 | bytes 1000000 | tf_op jit(solution)/shard_map/splat_side/pallas_call | solution.py:451
  19.5 0.0 collective-permute-done.3.near_target
  19.5 0.0 collective-permute-done.4.far_target
  19.5 5.2 %pull.1 = (f32[24,16,480]{2,1,0:T(8,128)}, f32[3,8,128]{2,1,0:T(8,128)S(1)}, f32[3,8,128]{2,1,0:T(8,128)S(1)}, f32[3,8,128]{2,1,0:T(8,128)S(1)}, f32[3,8,128]{2,1,0:T(8,128)S(1)}) custom-call(f32[4,5,8,128]{3,2,1,0:T(8,128)S(1)} %pad_maximum_fusion.refs_0_.atoms_ref, bf16[6,16,480]{2,1,0:T(8,128)(2,1)S(1)} %collective-permute-done.3.near_target, ...), custom_call_target="tpu_custom_call" | custom-call | flops 6000000000 | bytes 14000000 | tf_op jit(solution)/shard_map/pull/pallas_call | solution.py:474
  24.7 2.1 %collective-permute-start.7 = (f32[3,8,128]{2,1,0:T(8,128)S(1)}, f32[3,8,128]{2,1,0:T(8,128)S(1)}, u32[]{:S(2)}, u32[]{:S(2)}) collective-permute-start(f32[3,8,128]{2,1,0:T(8,128)S(1)} %get-tuple-element.33), channel_id=1, source_target_pairs={{0,8},{4,12},{8,0},{12,4},{1,9},{5,13},{9,1},{13,5},{2,10},{6,14},... | collective-permute-start | bytes 36872 | tf_op jit(solution)/shard_map/ppermute | solution.py:407
  26.8 0.0 collective-permute-start.8
  26.8 1.5 %collective-permute-start.9 = (f32[3,8,128]{2,1,0:T(8,128)S(1)}, f32[3,8,128]{2,1,0:T(8,128)S(1)}, u32[]{:S(2)}, u32[]{:S(2)}) collective-permute-start(f32[3,8,128]{2,1,0:T(8,128)S(1)} %get-tuple-element.35), channel_id=1, source_target_pairs={{0,4},{4,0},{8,12},{12,8},{1,5},{5,1},{9,13},{13,9},{2,6},{6,2},{1... | collective-permute-start | bytes 36872 | tf_op jit(solution)/shard_map/ppermute | solution.py:407
  28.3 1.2 %collective-permute-done.7 = f32[3,8,128]{2,1,0:T(8,128)S(1)} collective-permute-done((f32[3,8,128]{2,1,0:T(8,128)S(1)}, f32[3,8,128]{2,1,0:T(8,128)S(1)}, u32[]{:S(2)}, u32[]{:S(2)}) %collective-permute-start.7) | collective-permute-done | bytes 12320 | tf_op jit(solution)/shard_map/ppermute | solution.py:407
  29.4 2.9 %collective-permute-done.8 = f32[3,8,128]{2,1,0:T(8,128)S(1)} collective-permute-done((f32[3,8,128]{2,1,0:T(8,128)S(1)}, f32[3,8,128]{2,1,0:T(8,128)S(1)}, u32[]{:S(2)}, u32[]{:S(2)}) %collective-permute-start.8) | collective-permute-done | bytes 12320 | tf_op jit(solution)/shard_map/ppermute | solution.py:407
  32.3 0.0 collective-permute-done.9
  32.3 0.6 %add_add_fusion = f32[3,8,128]{2,1,0:T(8,128)} fusion(f32[3,8,128]{2,1,0:T(8,128)S(1)} %collective-permute-done.9, f32[3,8,128]{2,1,0:T(8,128)S(1)} %collective-permute-done.8, f32[3,8,128]{2,1,0:T(8,128)S(1)} %get-tuple-element.32, f32[3,8,128]{2,1,0:T(8,128)S(1)} %collective-permute-done.7), kind=kLoop, calls=%fused_computation.3 | loop fusion | flops 9216 | bytes 61440 | tf_op jit(solution)/shard_map/add | solution.py:497
  (1 shorter events, 0.0 us)
Async XLA Ops:
  2.0 6.9 %collective-permute-start.2 = (f32[5,8,128]{2,1,0:T(8,128)S(1)}, f32[5,8,128]{2,1,0:T(8,128)S(1)}, u32[]{:S(2)}, u32[]{:S(2)}) collective-permute-start(f32[5,8,128]{2,1,0:T(8,128)S(1)} %pack.1), channel_id=1, source_target_pairs={{0,12},{4,8},{8,4},{12,0},{1,13},{5,9},{9,5},{13,1},{2,14},{6,10},... | collective-permute-start | bytes 61448 | tf_op jit(solution)/shard_map/ppermute | solution.py:407
  7.1 4.7 %collective-permute-start.1 = (f32[5,8,128]{2,1,0:T(8,128)S(1)}, f32[5,8,128]{2,1,0:T(8,128)S(1)}, u32[]{:S(2)}, u32[]{:S(2)}) collective-permute-start(f32[5,8,128]{2,1,0:T(8,128)S(1)} %pack.1), channel_id=1, source_target_pairs={{0,8},{4,12},{8,0},{12,4},{1,9},{5,13},{9,1},{13,5},{2,10},{6,14},... | collective-permute-start | bytes 61448 | tf_op jit(solution)/shard_map/ppermute | solution.py:407
  7.2 4.7 %collective-permute-start = (f32[5,8,128]{2,1,0:T(8,128)S(1)}, f32[5,8,128]{2,1,0:T(8,128)S(1)}, u32[]{:S(2)}, u32[]{:S(2)}) collective-permute-start(f32[5,8,128]{2,1,0:T(8,128)S(1)} %pack.1), channel_id=1, source_target_pairs={{0,4},{4,0},{8,12},{12,8},{1,5},{5,1},{9,13},{13,9},{2,6},{6,2},{1... | collective-permute-start | bytes 61448 | tf_op jit(solution)/shard_map/ppermute | solution.py:407
  11.8 4.8 %collective-permute-start.6 = (f32[4,5,8,128]{3,2,1,0:T(8,128)S(1)}, f32[4,5,8,128]{3,2,1,0:T(8,128)S(1)}, u32[]{:S(2)}, u32[]{:S(2)}) collective-permute-start(f32[4,5,8,128]{3,2,1,0:T(8,128)S(1)} %pad_maximum_fusion.refs_0_.atoms_ref), channel_id=1, source_target_pairs={{1,2},{3,0},{2,1},{0,3},{5,6},{7,4},{6,5},{4,7},{9,10},{11,8},{10,... | collective-permute-start | bytes 245768 | tf_op jit(solution)/shard_map/ppermute | solution.py:399
  11.9 4.7 %collective-permute-start.5 = (f32[4,5,8,128]{3,2,1,0:T(8,128)S(1)}, f32[4,5,8,128]{3,2,1,0:T(8,128)S(1)}, u32[]{:S(2)}, u32[]{:S(2)}) collective-permute-start(f32[4,5,8,128]{3,2,1,0:T(8,128)S(1)} %pad_maximum_fusion.refs_0_.atoms_ref), channel_id=1, source_target_pairs={{0,1},{2,3},{1,0},{3,2},{4,5},{6,7},{5,4},{7,6},{8,9},{10,11},{9,8... | collective-permute-start | bytes 245768 | tf_op jit(solution)/shard_map/ppermute | solution.py:399
  13.5 6.0 %collective-permute-start.3 = (bf16[6,16,480]{2,1,0:T(8,128)(2,1)S(1)}, bf16[6,16,480]{2,1,0:T(8,128)(2,1)S(1)}, u32[]{:S(2)}, u32[]{:S(2)}) collective-permute-start(bf16[6,16,480]{2,1,0:T(8,128)(2,1)S(1)} %get-tuple-element.22), channel_id=1, source_target_pairs={{0,1},{2,3},{1,0},{3,2},{4,5},{6,7},{5,4},{7,6},{8,9},{10,11},{9,8... | collective-permute-start | bytes 276488 | tf_op jit(solution)/shard_map/ppermute | solution.py:399
  13.5 6.0 %collective-permute-start.4 = (bf16[6,16,480]{2,1,0:T(8,128)(2,1)S(1)}, bf16[6,16,480]{2,1,0:T(8,128)(2,1)S(1)}, u32[]{:S(2)}, u32[]{:S(2)}) collective-permute-start(bf16[6,16,480]{2,1,0:T(8,128)(2,1)S(1)} %get-tuple-element.23), channel_id=1, source_target_pairs={{1,2},{3,0},{2,1},{0,3},{5,6},{7,4},{6,5},{4,7},{9,10},{11,8},{10,... | collective-permute-start | bytes 276488 | tf_op jit(solution)/shard_map/ppermute | solution.py:399
  24.7 4.7 %collective-permute-start.7 = (f32[3,8,128]{2,1,0:T(8,128)S(1)}, f32[3,8,128]{2,1,0:T(8,128)S(1)}, u32[]{:S(2)}, u32[]{:S(2)}) collective-permute-start(f32[3,8,128]{2,1,0:T(8,128)S(1)} %get-tuple-element.33), channel_id=1, source_target_pairs={{0,8},{4,12},{8,0},{12,4},{1,9},{5,13},{9,1},{13,5},{2,10},{6,14},... | collective-permute-start | bytes 36872 | tf_op jit(solution)/shard_map/ppermute | solution.py:407
  26.8 5.5 %collective-permute-start.8 = (f32[3,8,128]{2,1,0:T(8,128)S(1)}, f32[3,8,128]{2,1,0:T(8,128)S(1)}, u32[]{:S(2)}, u32[]{:S(2)}) collective-permute-start(f32[3,8,128]{2,1,0:T(8,128)S(1)} %get-tuple-element.34), channel_id=1, source_target_pairs={{0,12},{4,8},{8,4},{12,0},{1,13},{5,9},{9,5},{13,1},{2,14},{6,10},... | collective-permute-start | bytes 36872 | tf_op jit(solution)/shard_map/ppermute | solution.py:407
  26.8 5.5 %collective-permute-start.9 = (f32[3,8,128]{2,1,0:T(8,128)S(1)}, f32[3,8,128]{2,1,0:T(8,128)S(1)}, u32[]{:S(2)}, u32[]{:S(2)}) collective-permute-start(f32[3,8,128]{2,1,0:T(8,128)S(1)} %get-tuple-element.35), channel_id=1, source_target_pairs={{0,4},{4,0},{8,12},{12,8},{1,5},{5,1},{9,13},{13,9},{2,6},{6,2},{1... | collective-permute-start | bytes 36872 | tf_op jit(solution)/shard_map/ppermute | solution.py:407
